TPU v7x, 32 devices: a whole 2x2x4 slice. The times are simulated.
32 devices in a mesh: member: 2 (over x), space: 16 (over z, y, core).
Axes of the slice: x: 2, y: 2, z: 4, core: 2. Of those that a mesh axis runs over, the one named last changes fastest.
Arguments:
- tangents: float32 [8, 4, 48, 64, 128], P('member', None, 'space'), parts along dimension 0, may hold values from -210 to 210
- background: float32 [6, 4, 48, 64, 128], P('member', None, 'space'), parts along dimension 0, may hold values from -3 to 3
- diffusivity: float32 [4], P('member'), parts along dimension 0, may hold values from 0.03 to 0.12
Outputs:
- basis: float32 [8, 4, 48, 64, 128], P('member', None, 'space'), parts along dimension 0
- growth: float32 [8, 4], P('member'), parts along dimension 0
There are 2 independent parts, one for each index of `member`. A program takes and returns all parts, laid end to end along the dimension named above; each array names one. Nothing has to cross between parts.
All inputs are finite; a program needn't handle non-finite values.
Results may differ from a plain program's by a relative error of at most 0.0003.
Values sent between devices are 32-bit elements; how exact they have to be, the bound alone decides.
A program may use at most 128 MiB of HBM per device.

v0:
```python
import jax
import jax.numpy as jnp
from jax import lax
from jax.sharding import PartitionSpec as P

STEP_DT = 0.25
BUOYANCY = 1.0


def extended(block, sides, width):
    for axis, dim in sides:
        count = lax.axis_size(axis)
        forward = [(i, i + 1) for i in range(count - 1)]
        backward = [(target, source) for source, target in forward]
        low = lax.ppermute(
            lax.slice_in_dim(block, block.shape[dim] - width, None, axis=dim), axis, forward
        )
        high = lax.ppermute(lax.slice_in_dim(block, 0, width, axis=dim), axis, backward)
        block = jnp.concatenate([low, block, high], axis=dim)
    return block


def inner(field):
    return field[..., 1:-1, :, :]


def slopes(field):
    slope_x = inner(jnp.roll(field, -1, axis=-1) - jnp.roll(field, 1, axis=-1)) * 0.5
    slope_y = inner(jnp.roll(field, -1, axis=-2) - jnp.roll(field, 1, axis=-2)) * 0.5
    slope_z = (field[..., 2:, :, :] - field[..., :-2, :, :]) * 0.5
    return (slope_x, slope_y, slope_z)


def laplace(field):
    sides = jnp.roll(field, -1, axis=-1) + jnp.roll(field, 1, axis=-1)
    sides = sides + jnp.roll(field, -1, axis=-2) + jnp.roll(field, 1, axis=-2)
    return inner(sides) + field[..., 2:, :, :] + field[..., :-2, :, :] - 6.0 * inner(field)


def tendency(tangent, ground, viscous, conduct):
    base_x, base_y, base_z = slopes(ground)
    flow = inner(ground)
    own_x, own_y, own_z = slopes(tangent)
    advect = flow[0] * own_x + flow[1] * own_y + flow[2] * own_z
    moving = inner(tangent)
    shear = (
        moving[:, 0:1] * base_x[None]
        + moving[:, 1:2] * base_y[None]
        + moving[:, 2:3] * base_z[None]
    )
    coeffs = jnp.stack([viscous, viscous, viscous, conduct]).reshape(4, 1, 1, 1)
    zeros = jnp.zeros_like(moving[:, 0:2])
    forcing = jnp.concatenate([zeros, BUOYANCY * moving[:, 3:4], moving[:, 2:3]], axis=1)
    return -advect - shear + coeffs * laplace(tangent) + forcing


def on_device(tangents, background, diffusivity):
    viscous = diffusivity[0]
    conduct = diffusivity[1]
    depth = 1
    ground = extended(background, (("space", 2),), depth)

    def section_rate(state, which):
        widened = extended(state, (("space", 2),), 1)
        return tendency(widened, ground[which], viscous, conduct)

    rate_one = section_rate(tangents, 0)
    rate_two = section_rate(tangents + STEP_DT * 0.5 * rate_one, 1)
    rate_three = section_rate(tangents + STEP_DT * 0.5 * rate_two, 1)
    rate_four = section_rate(tangents + STEP_DT * rate_three, 2)
    stepped = tangents + STEP_DT / 6.0 * (rate_one + 2.0 * rate_two + 2.0 * rate_three + rate_four)
    count = stepped.shape[0]
    flat = stepped.reshape(count, -1)
    rows_all = flat.shape[1] * lax.axis_size("space")
    gram = lax.psum(jnp.dot(flat, flat.T, precision=lax.Precision.HIGHEST), "space")
    lower_one = jnp.linalg.cholesky(gram)
    ortho_one = lax.linalg.triangular_solve(lower_one, flat, left_side=True, lower=True)
    factor = lower_one.T
    scale = jnp.sqrt(jnp.float32(rows_all))
    basis = (ortho_one * scale).reshape(stepped.shape)
    return (basis, factor / scale)


def solution(mesh):
    in_specs = (
        P("member", None, "space", None, None),
        P("member", None, "space", None, None),
        P("member"),
    )
    out_specs = (P("member", None, "space", None, None), P("member", None))
    return jax.shard_map(
        on_device, mesh=mesh, in_specs=in_specs, out_specs=out_specs, check_vma=False
    )
```

profile of v0, /device:TPU:0, one launch (start us, length us, event | category | flops | bytes accessed | tf_op | source)
XLA Modules:
  0.0 168.5 jit_solution(9535967832852833191)
XLA Ops:
  0.6 1.3 fusion.137
  2.0 1.3 collective-permute-start.3
  3.3 3.1 %collective-permute-start.2 = (f32[3,4,1,64,128]{4,3,2,1,0:T(8,128)S(1)}, f32[3,4,1,64,128]{4,3,2,1,0:T(8,128)S(1)}, u32[]{:S(2)}, u32[]{:S(2)}) collective-permute-start(f32[3,4,1,64,128]{4,3,2,1,0:T(8,128)S(1)} %get-tuple-element.74), channel_id=1, source_target_pairs={{0,1},{1,2},{2,3},{3,4},{4,5},{5,6},{6,7},{7,8},{8,9},{9,10},{10,1... | collective-permute-start | bytes 1179656 | tf_op jit(solution)/shard_map/ppermute | solution.py:15
  6.4 1.3 collective-permute-start.1
  7.7 5.3 %collective-permute-start = (f32[4,4,1,64,128]{4,3,2,1,0:T(8,128)S(1)}, f32[4,4,1,64,128]{4,3,2,1,0:T(8,128)S(1)}, u32[]{:S(2)}, u32[]{:S(2)}) collective-permute-start(f32[4,4,1,64,128]{4,3,2,1,0:T(8,128)S(1)} %get-tuple-element.72), channel_id=1, source_target_pairs={{0,1},{1,2},{2,3},{3,4},{4,5},{5,6},{6,7},{7,8},{8,9},{9,10},{10,1... | collective-permute-start | bytes 1572872 | tf_op jit(solution)/shard_map/ppermute | solution.py:15
  13.0 1.3 slice_bitcast_fusion.10
  15.9 0.8 fusion.114
  18.5 1.5 fusion.138
  20.0 1.5 fusion.139
  21.5 1.3 fusion.141
  22.8 1.0 fusion.105
  23.8 1.1 fusion.100
  25.0 1.1 fusion.101
  27.5 0.9 fusion.130
  28.5 0.9 fusion.129
  29.4 7.0 %multiply_add_fusion.2 = (f32[4,4,3,64,128]{4,3,2,1,0:T(8,128)S(1)}, f32[4,4,3,64,128]{4,3,2,1,0:T(8,128)}) fusion(f32[4,4,3,64,128]{4,3,2,1,0:T(8,128)S(1)} %copy-done, f32[4,1,3,64,128]{4,3,2,1,0:T(8,128)} %get-tuple-element.69, f32[4,1,3,64,128]{4,3,2,1,0:T(8,128)} %get-tuple-element.67, f32[4]{0:T(128)} %pad.70.clone, ...), kind=kLoop, calls=%fused_computation.141 | loop fusion | flops 15335424 | bytes 19693600 | tf_op jit(solution)/shard_map/add | solution.py:68
  36.6 8.8 %collective-permute-start.4 = (f32[4,4,1,64,128]{4,3,2,1,0:T(8,128)S(1)}, f32[4,4,1,64,128]{4,3,2,1,0:T(8,128)S(1)}, u32[]{:S(2)}, u32[]{:S(2)}) collective-permute-start(f32[4,4,1,64,128]{4,3,2,1,0:T(8,128)S(1)} %get-tuple-element.64), channel_id=1, source_target_pairs={{0,1},{1,2},{2,3},{3,4},{4,5},{5,6},{6,7},{7,8},{8,9},{9,10},{10,1... | collective-permute-start | bytes 1572872 | tf_op jit(solution)/shard_map/ppermute | solution.py:15
  45.4 1.5 collective-permute-start.5
  47.1 1.4 slice_bitcast_fusion.8
  48.5 2.7 %collective-permute-done.5 = f32[4,4,1,64,128]{4,3,2,1,0:T(8,128)S(1)} collective-permute-done((f32[4,4,1,64,128]{4,3,2,1,0:T(8,128)S(1)}, f32[4,4,1,64,128]{4,3,2,1,0:T(8,128)S(1)}, u32[]{:S(2)}, u32[]{:S(2)}) %collective-permute-start.5) | collective-permute-done | bytes 524320 | tf_op jit(solution)/shard_map/ppermute | solution.py:18
  52.0 0.9 fusion.128
  52.9 0.9 fusion.127
  53.9 1.0 fusion.5
  54.9 5.6 %multiply_add_fusion.1 = (f32[4,4,3,64,128]{4,3,2,1,0:T(8,128)S(1)}, f32[4,4,3,64,128]{4,3,2,1,0:T(8,128)}) fusion(f32[4,4,3,64,128]{4,3,2,1,0:T(8,128)S(1)} %copy-done, f32[4,1,3,64,128]{4,3,2,1,0:T(8,128)} %get-tuple-element.62, f32[4,1,3,64,128]{4,3,2,1,0:T(8,128)} %get-tuple-element.61, f32[4]{0:T(128)S(1)} %copy-done.15, ...), kind=kLoop, calls=%fused_computation.140 | loop fusion | flops 13762560 | bytes 19169312 | tf_op jit(solution)/shard_map/add | solution.py:69
  60.7 10.5 %collective-permute-start.6 = (f32[4,4,1,64,128]{4,3,2,1,0:T(8,128)S(1)}, f32[4,4,1,64,128]{4,3,2,1,0:T(8,128)S(1)}, u32[]{:S(2)}, u32[]{:S(2)}) collective-permute-start(f32[4,4,1,64,128]{4,3,2,1,0:T(8,128)S(1)} %get-tuple-element.57), channel_id=1, source_target_pairs={{0,1},{1,2},{2,3},{3,4},{4,5},{5,6},{6,7},{7,8},{8,9},{9,10},{10,1... | collective-permute-start | bytes 1572872 | tf_op jit(solution)/shard_map/ppermute | solution.py:15
  71.1 1.3 collective-permute-start.7
  72.5 1.1 fusion.95
  73.6 0.7 fusion.108
  74.3 1.5 slice_bitcast_fusion.6
  75.8 1.1 collective-permute-done.7
  77.7 0.9 fusion.125
  78.6 0.9 fusion.124
  79.6 2.5 %fusion.3 = (f32[4,4,5,64,128]{4,3,2,1,0:T(8,128)S(1)}, f32[4,4,5,64,128]{4,3,2,1,0:T(8,128)}) fusion(f32[4,4,1,64,128]{4,3,2,1,0:T(8,128)S(1)} %collective-permute-done.7, f32[4,4,3,64,128]{4,3,2,1,0:T(8,128)S(1)} %get-tuple-element.6, f32[4,4,1,64,128]{4,3,2,1,0:T(8,128)S(1)} %collective-permute-done.6, f32[4,4,5,63,128]{4,3,2,1,0:T(8,128)S(1)} %get-tuple-element.20, ...), kind=kLoop, calls=%fused_computation.11 | loop fusion | flops 3932160 | bytes 13025280 | tf_op jit(solution)/shard_map/jit(_roll_static)/concatenate | solution.py:29
  82.0 5.9 %multiply_add_fusion = (f32[4,4,3,64,128]{4,3,2,1,0:T(8,128)S(1)}, f32[4,4,3,64,128]{4,3,2,1,0:T(8,128)}) fusion(f32[4,4,3,64,128]{4,3,2,1,0:T(8,128)S(1)} %copy-done, f32[4,1,3,64,128]{4,3,2,1,0:T(8,128)} %get-tuple-element.55, f32[4,1,3,64,128]{4,3,2,1,0:T(8,128)} %get-tuple-element.54, f32[4]{0:T(128)S(1)} %copy-done.15, ...), kind=kLoop, calls=%fused_computation.139 | loop fusion | flops 13762560 | bytes 19169312 | tf_op jit(solution)/shard_map/add | solution.py:70
  88.0 10.5 %collective-permute-start.8 = (f32[4,4,1,64,128]{4,3,2,1,0:T(8,128)S(1)}, f32[4,4,1,64,128]{4,3,2,1,0:T(8,128)S(1)}, u32[]{:S(2)}, u32[]{:S(2)}) collective-permute-start(f32[4,4,1,64,128]{4,3,2,1,0:T(8,128)S(1)} %get-tuple-element.50), channel_id=1, source_target_pairs={{0,1},{1,2},{2,3},{3,4},{4,5},{5,6},{6,7},{7,8},{8,9},{9,10},{10,1... | collective-permute-start | bytes 1572872 | tf_op jit(solution)/shard_map/ppermute | solution.py:15
  98.5 1.5 collective-permute-start.9
  100.1 0.9 fusion.93
  101.0 0.8 fusion.91
  101.8 1.3 slice_bitcast_fusion.4
  103.1 1.2 collective-permute-done.9
  105.1 0.9 fusion.121
  106.0 0.9 fusion.122
  107.0 2.2 %fusion.1 = (f32[4,4,5,64,128]{4,3,2,1,0:T(8,128)S(1)}, f32[4,4,5,64,128]{4,3,2,1,0:T(8,128)}) fusion(f32[4,4,1,64,128]{4,3,2,1,0:T(8,128)S(1)} %collective-permute-done.9, f32[4,4,3,64,128]{4,3,2,1,0:T(8,128)S(1)} %get-tuple-element.4, f32[4,4,1,64,128]{4,3,2,1,0:T(8,128)S(1)} %collective-permute-done.8, f32[4,4,5,63,128]{4,3,2,1,0:T(8,128)S(1)} %get-tuple-element.12, ...), kind=kLoop, calls=%fused_computation.5 | loop fusion | flops 3932160 | bytes 13025280 | tf_op jit(solution)/shard_map/jit(_roll_static)/concatenate | solution.py:29
  109.2 6.0 %fusion.17 = f32[4,4,3,64,128]{4,3,2,1,0:T(8,128)S(1)} fusion(f32[4,4,3,64,128]{4,3,2,1,0:T(8,128)S(1)} %copy-done, f32[4,4,5,64,1]{4,3,2,1,0:T(8,128)S(1)} %get-tuple-element.15, f32[4,4,5,64,127]{4,3,2,1,0:T(8,128)S(1)} %get-tuple-element.17, f32[4,4,5,64,127]{4,3,2,1,0:T(8,128)S(1)} %get-tuple-element.16, f32[4,4,5,64,1]{4,3,2,1,0:T(8,128)S(1)} %get-tuple-element.14, ...), kind=kLoop, calls=%fused_computation.53 | loop fusion | flops 15728640 | bytes 22315040 | tf_op jit(solution)/shard_map/add | solution.py:71
  115.2 6.9 %fusion.88 = f32[4,4]{0,1:T(4,128)S(1)} fusion(f32[4,4,3,64,128]{4,3,2,1,0:T(8,128)S(1)} %fusion.17), kind=kOutput, calls=%fused_computation.143 | convolution fusion | flops 18874368 | bytes 1572928 | tf_op jit(solution)/shard_map/dot_general | solution.py:75
  122.0 38.2 %psum.7 = f32[4,4]{0,1:T(4,128)S(1)} all-reduce(f32[4,4]{0,1:T(4,128)S(1)} %fusion.88), channel_id=1, replica_groups=mesh['member'=2,'space'=16] {'space'}, use_global_device_ids=true, to_apply=%region_0.1 | all-reduce | flops 16 | bytes 128 | tf_op jit(solution)/shard_map/psum | solution.py:75
  163.0 4.3 %fusion.85 = f32[1,4,768,128]{3,1,2,0:T(4,128)S(1)} fusion(f32[1,4,768,128]{3,2,1,0:T(8,128)S(1)} %bitcast.74, f32[1,4,4]{1,2,0:T(4,128)S(1)} %custom-call.6), kind=kOutput, calls=%fused_computation.142 | convolution fusion | flops 19267584 | bytes 3145792 | tf_op jit(solution)/shard_map/triangular_solve | solution.py:77
  167.3 1.2 copy.14
  (83 shorter events, 10.6 us)
Async XLA Ops:
  0.6 5.7 %copy-start = (f32[4,4,3,64,128]{4,3,2,1,0:T(8,128)S(1)}, f32[4,4,3,64,128]{4,3,2,1,0:T(8,128)}, u32[]{:S(2)}) copy-start(f32[4,4,3,64,128]{4,3,2,1,0:T(8,128)} %param.3) | copy-start | bytes 4718596
  2.0 13.7 %collective-permute-start.3 = (f32[3,4,1,64,128]{4,3,2,1,0:T(8,128)S(1)}, f32[3,4,1,64,128]{4,3,2,1,0:T(8,128)S(1)}, u32[]{:S(2)}, u32[]{:S(2)}) collective-permute-start(f32[3,4,1,64,128]{4,3,2,1,0:T(8,128)S(1)} %get-tuple-element.73), channel_id=1, source_target_pairs={{1,0},{2,1},{3,2},{4,3},{5,4},{6,5},{7,6},{8,7},{9,8},{10,9},{11,1... | collective-permute-start | bytes 1179656 | tf_op jit(solution)/shard_map/ppermute | solution.py:18
  3.3 12.2 %collective-permute-start.2 = (f32[3,4,1,64,128]{4,3,2,1,0:T(8,128)S(1)}, f32[3,4,1,64,128]{4,3,2,1,0:T(8,128)S(1)}, u32[]{:S(2)}, u32[]{:S(2)}) collective-permute-start(f32[3,4,1,64,128]{4,3,2,1,0:T(8,128)S(1)} %get-tuple-element.74), channel_id=1, source_target_pairs={{0,1},{1,2},{2,3},{3,4},{4,5},{5,6},{6,7},{7,8},{8,9},{9,10},{10,1... | collective-permute-start | bytes 1179656 | tf_op jit(solution)/shard_map/ppermute | solution.py:15
  6.4 19.8 %collective-permute-start.1 = (f32[4,4,1,64,128]{4,3,2,1,0:T(8,128)S(1)}, f32[4,4,1,64,128]{4,3,2,1,0:T(8,128)S(1)}, u32[]{:S(2)}, u32[]{:S(2)}) collective-permute-start(f32[4,4,1,64,128]{4,3,2,1,0:T(8,128)S(1)} %get-tuple-element.71), channel_id=1, source_target_pairs={{1,0},{2,1},{3,2},{4,3},{5,4},{6,5},{7,6},{8,7},{9,8},{10,9},{11,1... | collective-permute-start | bytes 1572872 | tf_op jit(solution)/shard_map/ppermute | solution.py:18
  7.7 7.1 %copy-start.18 = (f32[2]{0:T(128)S(1)}, f32[2]{0:T(128)}, u32[]{:S(2)}) copy-start(f32[2]{0:T(128)} %param.5) | copy-start | bytes 28
  7.7 7.8 %copy-start.4 = (f32[3,4,3,64,128]{4,3,2,1,0:T(8,128)S(1)}, f32[3,4,3,64,128]{4,3,2,1,0:T(8,128)}, u32[]{:S(2)}) copy-start(f32[3,4,3,64,128]{4,3,2,1,0:T(8,128)} %param.4) | copy-start | bytes 3538948
  7.7 18.3 %collective-permute-start = (f32[4,4,1,64,128]{4,3,2,1,0:T(8,128)S(1)}, f32[4,4,1,64,128]{4,3,2,1,0:T(8,128)S(1)}, u32[]{:S(2)}, u32[]{:S(2)}) collective-permute-start(f32[4,4,1,64,128]{4,3,2,1,0:T(8,128)S(1)} %get-tuple-element.72), channel_id=1, source_target_pairs={{0,1},{1,2},{2,3},{3,4},{4,5},{5,6},{6,7},{7,8},{8,9},{9,10},{10,1... | collective-permute-start | bytes 1572872 | tf_op jit(solution)/shard_map/ppermute | solution.py:15
  36.5 10.5 %copy-start.13 = (f32[4,5,1,128]{3,2,1,0:T(1,128)S(1)}, f32[4,5,1,128]{3,2,1,0:T(1,128)}, u32[]{:S(2)}) copy-start(f32[4,5,1,128]{3,2,1,0:T(1,128)} %get-tuple-element.114) | copy-start | bytes 30724
  36.5 10.5 %copy-start.14 = (f32[4,5,1,128]{3,2,1,0:T(1,128)S(1)}, f32[4,5,1,128]{3,2,1,0:T(1,128)}, u32[]{:S(2)}) copy-start(f32[4,5,1,128]{3,2,1,0:T(1,128)} %get-tuple-element.115) | copy-start | bytes 30724
  36.6 11.9 %collective-permute-start.4 = (f32[4,4,1,64,128]{4,3,2,1,0:T(8,128)S(1)}, f32[4,4,1,64,128]{4,3,2,1,0:T(8,128)S(1)}, u32[]{:S(2)}, u32[]{:S(2)}) collective-permute-start(f32[4,4,1,64,128]{4,3,2,1,0:T(8,128)S(1)} %get-tuple-element.64), channel_id=1, source_target_pairs={{0,1},{1,2},{2,3},{3,4},{4,5},{5,6},{6,7},{7,8},{8,9},{9,10},{10,1... | collective-permute-start | bytes 1572872 | tf_op jit(solution)/shard_map/ppermute | solution.py:15
  45.4 5.8 %collective-permute-start.5 = (f32[4,4,1,64,128]{4,3,2,1,0:T(8,128)S(1)}, f32[4,4,1,64,128]{4,3,2,1,0:T(8,128)S(1)}, u32[]{:S(2)}, u32[]{:S(2)}) collective-permute-start(f32[4,4,1,64,128]{4,3,2,1,0:T(8,128)S(1)} %get-tuple-element.65), channel_id=1, source_target_pairs={{1,0},{2,1},{3,2},{4,3},{5,4},{6,5},{7,6},{8,7},{9,8},{10,9},{11,1... | collective-permute-start | bytes 1572872 | tf_op jit(solution)/shard_map/ppermute | solution.py:18
  53.9 1.0 copy-start.11
  53.9 1.0 copy-start.15
  53.9 1.0 copy-start.16
  54.9 17.5 %copy-start.10 = (f32[4,5,64,127]{3,2,1,0:T(8,128)S(1)}, f32[4,5,64,127]{3,2,1,0:T(8,128)}, u32[]{:S(2)}) copy-start(f32[4,5,64,127]{3,2,1,0:T(8,128)} %get-tuple-element.81) | copy-start | bytes 1950724
  60.5 11.9 %copy-start.7 = (f32[4,5,64,1]{3,2,1,0:T(8,128)S(1)}, f32[4,5,64,1]{3,2,1,0:T(8,128)}, u32[]{:S(2)}) copy-start(f32[4,5,64,1]{3,2,1,0:T(8,128)} %get-tuple-element.78) | copy-start | bytes 15364
  60.5 11.9 %copy-start.8 = (f32[4,5,64,1]{3,2,1,0:T(8,128)S(1)}, f32[4,5,64,1]{3,2,1,0:T(8,128)}, u32[]{:S(2)}) copy-start(f32[4,5,64,1]{3,2,1,0:T(8,128)} %get-tuple-element.79) | copy-start | bytes 15364
  60.5 11.9 %copy-start.9 = (f32[4,5,64,127]{3,2,1,0:T(8,128)S(1)}, f32[4,5,64,127]{3,2,1,0:T(8,128)}, u32[]{:S(2)}) copy-start(f32[4,5,64,127]{3,2,1,0:T(8,128)} %get-tuple-element.80) | copy-start | bytes 1950724
  60.7 15.1 %collective-permute-start.6 = (f32[4,4,1,64,128]{4,3,2,1,0:T(8,128)S(1)}, f32[4,4,1,64,128]{4,3,2,1,0:T(8,128)S(1)}, u32[]{:S(2)}, u32[]{:S(2)}) collective-permute-start(f32[4,4,1,64,128]{4,3,2,1,0:T(8,128)S(1)} %get-tuple-element.57), channel_id=1, source_target_pairs={{0,1},{1,2},{2,3},{3,4},{4,5},{5,6},{6,7},{7,8},{8,9},{9,10},{10,1... | collective-permute-start | bytes 1572872 | tf_op jit(solution)/shard_map/ppermute | solution.py:15
  71.1 5.8 %collective-permute-start.7 = (f32[4,4,1,64,128]{4,3,2,1,0:T(8,128)S(1)}, f32[4,4,1,64,128]{4,3,2,1,0:T(8,128)S(1)}, u32[]{:S(2)}, u32[]{:S(2)}) collective-permute-start(f32[4,4,1,64,128]{4,3,2,1,0:T(8,128)S(1)} %get-tuple-element.58), channel_id=1, source_target_pairs={{1,0},{2,1},{3,2},{4,3},{5,4},{6,5},{7,6},{8,7},{9,8},{10,9},{11,1... | collective-permute-start | bytes 1572872 | tf_op jit(solution)/shard_map/ppermute | solution.py:18
  87.9 12.1 %copy-start.5 = (f32[4,5,63,128]{3,2,1,0:T(8,128)S(1)}, f32[4,5,63,128]{3,2,1,0:T(8,128)}, u32[]{:S(2)}) copy-start(f32[4,5,63,128]{3,2,1,0:T(8,128)} %get-tuple-element.84) | copy-start | bytes 1935364
  87.9 12.2 %copy-start.6 = (f32[4,5,63,128]{3,2,1,0:T(8,128)S(1)}, f32[4,5,63,128]{3,2,1,0:T(8,128)}, u32[]{:S(2)}) copy-start(f32[4,5,63,128]{3,2,1,0:T(8,128)} %get-tuple-element.85) | copy-start | bytes 1935364
  87.9 12.2 %copy-start.12 = (f32[4,5,1,128]{3,2,1,0:T(1,128)S(1)}, f32[4,5,1,128]{3,2,1,0:T(1,128)}, u32[]{:S(2)}) copy-start(f32[4,5,1,128]{3,2,1,0:T(1,128)} %get-tuple-element.83) | copy-start | bytes 30724
  88.0 15.0 %collective-permute-start.8 = (f32[4,4,1,64,128]{4,3,2,1,0:T(8,128)S(1)}, f32[4,4,1,64,128]{4,3,2,1,0:T(8,128)S(1)}, u32[]{:S(2)}, u32[]{:S(2)}) collective-permute-start(f32[4,4,1,64,128]{4,3,2,1,0:T(8,128)S(1)} %get-tuple-element.50), channel_id=1, source_target_pairs={{0,1},{1,2},{2,3},{3,4},{4,5},{5,6},{6,7},{7,8},{8,9},{9,10},{10,1... | collective-permute-start | bytes 1572872 | tf_op jit(solution)/shard_map/ppermute | solution.py:15
  98.5 5.8 %collective-permute-start.9 = (f32[4,4,1,64,128]{4,3,2,1,0:T(8,128)S(1)}, f32[4,4,1,64,128]{4,3,2,1,0:T(8,128)S(1)}, u32[]{:S(2)}, u32[]{:S(2)}) collective-permute-start(f32[4,4,1,64,128]{4,3,2,1,0:T(8,128)S(1)} %get-tuple-element.51), channel_id=1, source_target_pairs={{1,0},{2,1},{3,2},{4,3},{5,4},{6,5},{7,6},{8,7},{9,8},{10,9},{11,1... | collective-permute-start | bytes 1572872 | tf_op jit(solution)/shard_map/ppermute | solution.py:18
  103.1 3.9 %copy-start.2 = (f32[4,4,1,64,128]{4,3,2,1,0:T(8,128)}, f32[4,4,1,64,128]{4,3,2,1,0:T(8,128)S(1)}, u32[]{:S(2)}) copy-start(f32[4,4,1,64,128]{4,3,2,1,0:T(8,128)S(1)} %collective-permute-done.8) | copy-start | bytes 1572868
  104.3 2.7 %copy-start.3 = (f32[4,4,1,64,128]{4,3,2,1,0:T(8,128)}, f32[4,4,1,64,128]{4,3,2,1,0:T(8,128)S(1)}, u32[]{:S(2)}) copy-start(f32[4,4,1,64,128]{4,3,2,1,0:T(8,128)S(1)} %collective-permute-done.9) | copy-start | bytes 1572868
  107.0 2.2 %copy-start.1 = (f32[4,4,3,64,128]{4,3,2,1,0:T(8,128)S(1)}, f32[4,4,3,64,128]{4,3,2,1,0:T(8,128)}, u32[]{:S(2)}) copy-start(f32[4,4,3,64,128]{4,3,2,1,0:T(8,128)} %get-tuple-element.7) | copy-start | bytes 4718596
  107.0 2.2 %copy-start.17 = (f32[4]{0:T(128)S(1)}, f32[4]{0:T(128)}, u32[]{:S(2)}) copy-start(f32[4]{0:T(128)} %pad_maximum_fusion.45) | copy-start | bytes 52
where the time goes:
time: 169 us
  starting transfers between devices  45 us (27%)
  other arithmetic  41.5 us (25%)
  blocking collectives  38.2 us (23%)
  local copies, waits for them, and re-layouts  26.4 us (16%)
  matrix products  11.1 us (7%)
  waiting for transfers between devices  5.09 us (3%)
    psum x1, blocking collectives, on_device(): lax.psum(jnp.dot(flat, flat.T, precision=lax.Precision.HIGHEST), 'space')  38.2 us
    ppermute x5, starting transfers between devices, extended(): lax.ppermute(lax.slice_in_dim(block, block.shape[dim] - width, None, axis...  38.1 us
    slice x8, local copies, waits for them, and re-layouts, slopes(): jnp.roll(field, -1, axis=-1) - jnp.roll(field, 1, axis=-1)  7.51 us
    add x1, other arithmetic, on_device(): rate_two = section_rate(tangents + STEP_DT * 0.5 * rate_one, 1)  7.02 us
    dot_general x1, matrix products, on_device(): jnp.dot(flat, flat.T, precision=lax.Precision.HIGHEST)  6.87 us
    ppermute x5, starting transfers between devices, extended(): lax.ppermute(lax.slice_in_dim(block, 0, width, axis=dim), axis, backward)  6.86 us
    add x1, other arithmetic, on_device(): tangents + STEP_DT / 6.0 * (rate_one + 2.0 * rate_two + 2.0 * rate_three...  5.96 us
    add x1, other arithmetic, on_device(): rate_four = section_rate(tangents + STEP_DT * rate_three, 2)  5.88 us
  transfers between devices with their start and end apart: 10, of which 3 were waited for; matrix products, arithmetic and copies ran while one was open for 12% of the time, Pallas kernels for 0%

commit v1 on v0

v1 whole, which is shorter than its diff:
```python
import functools
import jax
import jax.numpy as jnp
from jax import lax
from jax.experimental import pallas as pl
from jax.experimental.pallas import tpu as pltpu
from jax.sharding import PartitionSpec as P

STEP_DT = 0.25
BUOYANCY = 1.0
MESH = pl.DeviceIdType.MESH
PAD = 8
ROWS = 16
PAIRS = [(i, j) for j in range(4) for i in range(j + 1)]


def step_kernel(
    space,
    t_hbm,
    b_hbm,
    diff,
    stepped,
    coef_out,
    y0,
    y1,
    y2,
    y3,
    base,
    base_lo,
    base_hi,
    lo,
    hi,
    coef,
    grams,
    local_sem,
    send_sem,
    recv_sem,
    base_send,
    base_recv,
    gram_send,
    gram_recv,
):
    vectors, comps, depth, ny, nx = t_hbm.shape
    states = b_hbm.shape[0]
    last = depth - 1
    me = lax.axis_index("space")
    upper = lax.rem(me + 1, space)
    lower = lax.rem(me + space - 1, space)
    has_lower = me > 0
    has_upper = me < space - 1
    ys = [y0, y1, y2, y3]
    nu, kappa = diff[0], diff[1]

    def local_copies():
        out = []
        for k, (src, dst) in enumerate(((b_hbm, base), (t_hbm, y0))):
            for m, (a, b, rows) in enumerate(
                ((0, PAD, ny), (ny - PAD, 0, PAD), (0, PAD + ny, PAD))
            ):
                out.append(
                    pltpu.make_async_copy(
                        src.at[:, :, :, pl.ds(a, rows), :],
                        dst.at[:, :, :, pl.ds(b, rows), :],
                        local_sem.at[k, m],
                    )
                )
        return out

    def base_up(b):
        return pltpu.make_async_remote_copy(
            b_hbm.at[b, :, last], base_lo.at[b], base_send.at[0, b], base_recv.at[0, b],
            device_id={"space": upper}, device_id_type=MESH,
        )

    def base_down(b):
        return pltpu.make_async_remote_copy(
            b_hbm.at[b, :, 0], base_hi.at[b], base_send.at[1, b], base_recv.at[1, b],
            device_id={"space": lower}, device_id_type=MESH,
        )

    def state_plane(s, j, p):
        if s == 0:
            return t_hbm.at[j, :, p]
        return ys[s].at[j, :, p, pl.ds(PAD, ny), :]

    def send_up(s, j):
        return pltpu.make_async_remote_copy(
            state_plane(s, j, last), lo.at[s, j], send_sem.at[0, s, j], recv_sem.at[0, s, j],
            device_id={"space": upper}, device_id_type=MESH,
        )

    def send_down(s, j):
        return pltpu.make_async_remote_copy(
            state_plane(s, j, 0), hi.at[s, j], send_sem.at[1, s, j], recv_sem.at[1, s, j],
            device_id={"space": lower}, device_id_type=MESH,
        )

    def both(up, down, *key, op):
        @pl.when(has_upper)
        def _():
            getattr(up(*key), op)()

        @pl.when(has_lower)
        def _():
            getattr(down(*key), op)()

    def receive(up, down, *key):
        @pl.when(has_lower)
        def _():
            up(*key).wait_recv()

        @pl.when(has_upper)
        def _():
            down(*key).wait_recv()

    copies = local_copies()
    for c in copies:
        c.start()

    barrier = pltpu.get_barrier_semaphore()

    @pl.loop(1, space)
    def _(d):
        pl.semaphore_signal(
            barrier, inc=1, device_id={"space": lax.rem(me + d, space)}, device_id_type=MESH
        )

    pl.semaphore_wait(barrier, space - 1)

    both(base_up, base_down, 0, op="start")

    @pl.loop(0, vectors)
    def _(j):
        both(send_up, send_down, 0, j, op="start")

    both(base_up, base_down, 1, op="start")

    @pl.when(jnp.logical_not(has_lower))
    def _():
        base_lo[...] = jnp.zeros_like(base_lo)

        @pl.loop(0, vectors)
        def _(j):
            for s in range(4):
                lo[s, j] = jnp.zeros(lo.shape[2:], jnp.float32)

    @pl.when(jnp.logical_not(has_upper))
    def _():
        base_hi[...] = jnp.zeros_like(base_hi)

        @pl.loop(0, vectors)
        def _(j):
            for s in range(4):
                hi[s, j] = jnp.zeros(hi.shape[2:], jnp.float32)

    for c in copies:
        c.wait()

    def x_sides(q):
        return pltpu.roll(q, nx - 1, 1), pltpu.roll(q, 1, 1)

    def base_coeffs(b, p):
        @pl.loop(0, ny, step=ROWS)
        def _(r):
            r = pl.multiple_of(r, ROWS)
            here = pl.ds(r, ROWS)
            for c in range(comps):
                q = base[b, c, p, pl.ds(PAD + r, ROWS), :]
                right, left = x_sides(q)
                front = base[b, c, p, pl.ds(PAD + 1 + r, ROWS), :]
                back = base[b, c, p, pl.ds(PAD - 1 + r, ROWS), :]
                if p == 0:
                    below = base_lo[b, c, here, :]
                else:
                    below = base[b, c, p - 1, pl.ds(PAD + r, ROWS), :]
                if p == last:
                    above = base_hi[b, c, here, :]
                else:
                    above = base[b, c, p + 1, pl.ds(PAD + r, ROWS), :]
                if c < 3:
                    coef[b, p, c, here, :] = -0.5 * q
                coef[b, p, 3 + 3 * c, here, :] = 0.5 * (left - right)
                coef[b, p, 4 + 3 * c, here, :] = 0.5 * (back - front)
                coef[b, p, 5 + 3 * c, here, :] = 0.5 * (below - above)

    def advance(s, b, j, p):
        y = ys[s]

        @pl.loop(0, ny, step=ROWS)
        def _(r):
            r = pl.multiple_of(r, ROWS)
            here = pl.ds(r, ROWS)
            mid = pl.ds(PAD + r, ROWS)
            qs = [y[j, c, p, mid, :] for c in range(comps)]
            flow = [coef[b, p, d, here, :] for d in range(3)]
            for c in range(comps):
                q = qs[c]
                right, left = x_sides(q)
                front = y[j, c, p, pl.ds(PAD + 1 + r, ROWS), :]
                back = y[j, c, p, pl.ds(PAD - 1 + r, ROWS), :]
                below = lo[s, j, c, here, :] if p == 0 else y[j, c, p - 1, mid, :]
                above = hi[s, j, c, here, :] if p == last else y[j, c, p + 1, mid, :]
                rate = (
                    flow[0] * (right - left) + flow[1] * (front - back) + flow[2] * (above - below)
                )
                for d in range(3):
                    rate = rate + qs[d] * coef[b, p, 3 + 3 * c + d, here, :]
                around = (right + left) + (front + back) + (above + below)
                rate = rate + (kappa if c == 3 else nu) * (around - 6.0 * q)
                if c == 2:
                    rate = rate + BUOYANCY * qs[3]
                if c == 3:
                    rate = rate + qs[2]
                if s < 3:
                    start = q if s == 0 else y0[j, c, p, mid, :]
                    step = STEP_DT if s == 2 else STEP_DT * 0.5
                    ys[s + 1][j, c, p, mid, :] = start + step * rate
                else:
                    sums = (
                        y1[j, c, p, mid, :] + 2.0 * y2[j, c, p, mid, :] + (q - y0[j, c, p, mid, :])
                    )
                    stepped[j, c, p, here, :] = (1.0 / 3.0) * sums + (STEP_DT / 6.0) * rate

        if s < 3:
            nxt = ys[s + 1]
            for c in range(comps):
                nxt[j, c, p, pl.ds(0, PAD), :] = nxt[j, c, p, pl.ds(ny, PAD), :]
                nxt[j, c, p, pl.ds(PAD + ny, PAD), :] = nxt[j, c, p, pl.ds(PAD, PAD), :]

    inside = range(1, last)
    outside = [0, last] if last > 0 else [0]

    for p in inside:
        base_coeffs(0, p)
    receive(base_up, base_down, 0)
    for p in outside:
        base_coeffs(0, p)

    which = [0, 1, 1, 2]
    for s in range(4):
        if s == 1:
            receive(base_up, base_down, 1)
            for p in range(depth):
                base_coeffs(1, p)
        if s == 3:
            receive(base_up, base_down, 2)
            for p in range(depth):
                base_coeffs(2, p)

        @pl.loop(0, vectors)
        def _(j):
            receive(send_up, send_down, s, j)
            for p in outside:
                advance(s, which[s], j, p)
            if s < 3:
                both(send_up, send_down, s + 1, j, op="start")
            for p in inside:
                advance(s, which[s], j, p)

        if s == 1:
            both(base_up, base_down, 2, op="start")

    zero = jnp.zeros((ROWS, nx), jnp.float32)
    sums = (zero,) * len(PAIRS)
    for p in range(depth):
        def body(k, sums, p=p):
            r = pl.multiple_of(k * ROWS, ROWS)
            for c in range(comps):
                q = [stepped[j, c, p, pl.ds(r, ROWS), :] for j in range(vectors)]
                sums = tuple(a + q[i] * q[j] for a, (i, j) in zip(sums, PAIRS))
            return sums

        sums = lax.fori_loop(0, ny // ROWS, body, sums)
    rows = [jnp.sum(a, axis=0, keepdims=True) for a in sums]
    rows += [jnp.zeros((1, nx), jnp.float32)] * (16 - len(rows))
    grams[me] = jnp.concatenate(rows, axis=0)

    def gram_copy(d):
        return pltpu.make_async_remote_copy(
            grams.at[me], grams.at[me], gram_send.at[d], gram_recv.at[d],
            device_id={"space": lax.rem(me + d, space)}, device_id_type=MESH,
        )

    def gram_arrival(d):
        source = lax.rem(me + space - d, space)
        return pltpu.make_async_remote_copy(
            grams.at[source], grams.at[source], gram_send.at[d], gram_recv.at[d],
            device_id={"space": lax.rem(me + d, space)}, device_id_type=MESH,
        )

    @pl.loop(1, space)
    def _(d):
        gram_copy(d).start()

    @pl.loop(1, space)
    def _(d):
        gram_arrival(d).wait_recv()

    total = lax.fori_loop(0, space, lambda d, a: a + grams[d], jnp.zeros((16, nx), jnp.float32))
    total = jnp.broadcast_to(jnp.sum(total, axis=1, keepdims=True), (16, nx))
    gram = {pair: total[k : k + 1, :] for k, pair in enumerate(PAIRS)}

    low, inv = {}, {}
    recip = {}
    for k in range(vectors):
        rest = gram[k, k]
        for m in range(k):
            rest = rest - low[k, m] * low[k, m]
        low[k, k] = jnp.sqrt(rest)
        recip[k] = 1.0 / low[k, k]
        for i in range(k + 1, vectors):
            rest = gram[k, i]
            for m in range(k):
                rest = rest - low[i, m] * low[k, m]
            low[i, k] = rest * recip[k]
    for k in range(vectors):
        inv[k, k] = recip[k]
        for i in range(k + 1, vectors):
            rest = low[i, k] * inv[k, k]
            for m in range(k + 1, i):
                rest = rest + low[i, m] * inv[m, k]
            inv[i, k] = -rest * recip[i]
    blank = jnp.zeros((1, nx), jnp.float32)
    rows = [inv.get((i, k), blank) for i in range(vectors) for k in range(vectors)]
    rows += [low.get((k, i), blank) for i in range(vectors) for k in range(vectors)]
    coef_out[...] = jnp.concatenate(rows, axis=0)

    for b in range(states):
        both(base_up, base_down, b, op="wait_send")
    for s in range(4):
        @pl.loop(0, vectors)
        def _(j):
            both(send_up, send_down, s, j, op="wait_send")

    @pl.loop(1, space)
    def _(d):
        gram_copy(d).wait_send()


def basis_kernel(count, stepped, coef, basis, growth):
    vectors, _, depth, ny, nx = stepped.shape
    scale = jnp.sqrt(jnp.float32(count))
    comp = pl.program_id(0)

    def row(k):
        return jnp.broadcast_to(coef[k : k + 1, :], (8, nx))

    mix = {(i, k): scale * row(i * vectors + k) for i in range(vectors) for k in range(i + 1)}
    for p in range(depth):
        for r in range(0, ny, 8):
            q = [stepped[k, comp, p, r : r + 8, :] for k in range(vectors)]
            for i in range(vectors):
                total = mix[i, 0] * q[0]
                for k in range(1, i + 1):
                    total = total + mix[i, k] * q[k]
                basis[i, 0, p, r : r + 8, :] = total

    @pl.when(comp == 0)
    def _():
        lane = lax.broadcasted_iota(jnp.int32, (1, nx), 1)
        rows = []
        for i in range(vectors):
            out = jnp.zeros((1, nx), jnp.float32)
            for k in range(vectors):
                at = vectors * vectors + i * vectors + k
                out = jnp.where(lane == k, coef[at : at + 1, :], out)
            rows.append(out)
        growth[...] = (jnp.concatenate(rows, axis=0) / scale)[:, :vectors]


def on_device(tangents, background, diffusivity):
    space = lax.axis_size("space")
    vectors, comps, depth, ny, nx = tangents.shape
    states = background.shape[0]
    f32 = jnp.float32
    padded = ny + 2 * PAD
    vmem = pl.BlockSpec(memory_space=pltpu.VMEM)
    hbm = pl.BlockSpec(memory_space=pl.ANY)
    stepped, coef = pl.pallas_call(
        functools.partial(step_kernel, space),
        out_shape=(
            jax.ShapeDtypeStruct(tangents.shape, f32),
            jax.ShapeDtypeStruct((2 * vectors * vectors, nx), f32),
        ),
        in_specs=[hbm, hbm, pl.BlockSpec(memory_space=pltpu.SMEM)],
        out_specs=(vmem, vmem),
        scratch_shapes=[pltpu.VMEM((vectors, comps, depth, padded, nx), f32)] * 4
        + [
            pltpu.VMEM((states, comps, depth, padded, nx), f32),
            pltpu.VMEM((states, comps, ny, nx), f32),
            pltpu.VMEM((states, comps, ny, nx), f32),
            pltpu.VMEM((4, vectors, comps, ny, nx), f32),
            pltpu.VMEM((4, vectors, comps, ny, nx), f32),
            pltpu.VMEM((states, depth, 15, ny, nx), f32),
            pltpu.VMEM((space, 16, nx), f32),
            pltpu.SemaphoreType.DMA((2, 3)),
            pltpu.SemaphoreType.DMA((2, 4, vectors)),
            pltpu.SemaphoreType.DMA((2, 4, vectors)),
            pltpu.SemaphoreType.DMA((2, states)),
            pltpu.SemaphoreType.DMA((2, states)),
            pltpu.SemaphoreType.DMA((space,)),
            pltpu.SemaphoreType.DMA((space,)),
        ],
        compiler_params=pltpu.CompilerParams(
            collective_id=0, has_side_effects=True, vmem_limit_bytes=48 * 1024 * 1024
        ),
        name="tangent_step",
    )(tangents, background, diffusivity)
    block = (vectors, 1, depth, ny, nx)
    return pl.pallas_call(
        functools.partial(basis_kernel, tangents[0].size * space),
        grid=(comps,),
        out_shape=(
            jax.ShapeDtypeStruct(tangents.shape, f32),
            jax.ShapeDtypeStruct((vectors, vectors), f32),
        ),
        in_specs=[vmem, vmem],
        out_specs=(pl.BlockSpec(block, lambda c: (0, c, 0, 0, 0)), vmem),
        compiler_params=pltpu.CompilerParams(vmem_limit_bytes=16 * 1024 * 1024),
        name="basis",
    )(stepped, coef)


def solution(mesh):
    in_specs = (
        P("member", None, "space", None, None),
        P("member", None, "space", None, None),
        P("member"),
    )
    out_specs = (P("member", None, "space", None, None), P("member", None))
    return jax.shard_map(
        on_device, mesh=mesh, in_specs=in_specs, out_specs=out_specs, check_vma=False
    )
```

time: 169 us -> 74.9 us (0.44)
  Pallas kernels: 0 us -> 70.8 us
  starting transfers between devices: 45 us -> 0 us
  other arithmetic: 41.5 us -> 0 us
  blocking collectives: 38.2 us -> 0 us
  local copies, waits for them, and re-layouts: 26.4 us -> 3.33 us
  matrix products: 11.1 us -> 0 us
  waiting for transfers between devices: 5.09 us -> 0 us
    pallas_call x0 -> x2, Pallas kernels: none -> 70.8 us  [the longest x1 69 us: on_device(): pl.pallas_call(functools.partial(step_kernel, space), out_shape=(jax.Shap...]
    ppermute x10 -> x0, starting transfers between devices: 45 us -> none  [the longest x5 38.1 us: extended(): lax.ppermute(lax.slice_in_dim(block, block.shape[dim] - width, None, axis...]
    psum x1 -> x0, blocking collectives: 38.2 us -> none  [on_device(): lax.psum(jnp.dot(flat, flat.T, precision=lax.Precision.HIGHEST), 'space')]
    add x4 -> x0, other arithmetic: 24.5 us -> none  [the longest x1 7.02 us: on_device(): rate_two = section_rate(tangents + STEP_DT * 0.5 * rate_one, 1)]
    slice x26 -> x0, local copies, waits for them, and re-layouts: 17.8 us -> none  [the longest x8 7.51 us: slopes(): jnp.roll(field, -1, axis=-1) - jnp.roll(field, 1, axis=-1)]
    mul x11 -> x0, other arithmetic: 8.25 us -> none  [the longest x3 3.17 us: slopes(): inner(jnp.roll(field, -1, axis=-1) - jnp.roll(field, 1, axis=-1)) * 0.5]
    dot_general x1 -> x0, matrix products: 6.87 us -> none  [on_device(): jnp.dot(flat, flat.T, precision=lax.Precision.HIGHEST)]
    concatenate x6 -> x0, other arithmetic: 6.14 us -> none  [the longest x3 5.6 us: slopes(): jnp.roll(field, -1, axis=-2) - jnp.roll(field, 1, axis=-2)]
  transfers between devices with their start and end apart: 10 -> 0, of which waited for: 3 -> 0; matrix products, arithmetic and copies ran while one was open for 12% -> 0% of each run, Pallas kernels for 0% -> 0%
where the time goes in v1:
time: 74.9 us; the launch traced here: 74.7 us
  Pallas kernels  70.8 us (95%)
  local copies, waits for them, and re-layouts  3.33 us (4%)
    pallas_call x1, Pallas kernels, on_device(): pl.pallas_call(functools.partial(step_kernel, space), out_shape=(jax.Shap...  69 us
    unnamed x6, local copies, waits for them, and re-layouts  3.33 us
    pallas_call x1, Pallas kernels, on_device(): pl.pallas_call(functools.partial(basis_kernel, tangents[0].size * space),...  1.77 us

profile of v1, /device:TPU:0, one launch (start us, length us, event | category | flops | bytes accessed | tf_op | source)
XLA Modules:
  0.0 74.7 jit_solution(7457949970559103486)
XLA Ops:
  0.6 0.0 copy-start
  0.6 1.4 %copy-done = f32[4,4,3,64,128]{4,3,2,1,0:T(8,128)S(1)} copy-done((f32[4,4,3,64,128]{4,3,2,1,0:T(8,128)S(1)}, f32[4,4,3,64,128]{4,3,2,1,0:T(8,128)}, u32[]{:S(2)}) %copy-start) | copy-done | bytes 1572888
  2.0 0.0 copy-start.1
  2.0 1.3 %copy-done.1 = f32[3,4,3,64,128]{4,3,2,1,0:T(8,128)S(1)} copy-done((f32[3,4,3,64,128]{4,3,2,1,0:T(8,128)S(1)}, f32[3,4,3,64,128]{4,3,2,1,0:T(8,128)}, u32[]{:S(2)}) %copy-start.1) | copy-done | bytes 1179672
  3.3 0.0 copy-start.2
  3.3 0.7 copy-done.2
  4.0 69.0 %tangent_step.1 = (f32[4,4,3,64,128]{4,3,2,1,0:T(8,128)S(1)}, f32[32,128]{1,0:T(8,128)S(1)}) custom-call(f32[4,4,3,64,128]{4,3,2,1,0:T(8,128)S(1)} %copy-done, f32[3,4,3,64,128]{4,3,2,1,0:T(8,128)S(1)} %copy-done.1, f32[2]{0:T(128)S(1)} %copy-done.2), custom_call_target="tpu_custom_call" | custom-call | tf_op jit(solution)/shard_map/tangent_step/pallas_call | solution.py:379
  73.0 1.8 %basis.1 = (f32[4,4,3,64,128]{4,3,2,1,0:T(8,128)}, f32[4,4]{1,0:T(4,128)}) custom-call(f32[4,4,3,64,128]{4,3,2,1,0:T(8,128)S(1)} %get-tuple-element.4.stepped, f32[32,128]{1,0:T(8,128)S(1)} %get-tuple-element.5.coef), custom_call_target="tpu_custom_call" | custom-call | tf_op jit(solution)/shard_map/basis/pallas_call | solution.py:410
Async XLA Ops:
  0.6 1.4 %copy-start = (f32[4,4,3,64,128]{4,3,2,1,0:T(8,128)S(1)}, f32[4,4,3,64,128]{4,3,2,1,0:T(8,128)}, u32[]{:S(2)}) copy-start(f32[4,4,3,64,128]{4,3,2,1,0:T(8,128)} %t_hbm.1) | copy-start | bytes 4718596
  2.0 1.3 %copy-start.1 = (f32[3,4,3,64,128]{4,3,2,1,0:T(8,128)S(1)}, f32[3,4,3,64,128]{4,3,2,1,0:T(8,128)}, u32[]{:S(2)}) copy-start(f32[3,4,3,64,128]{4,3,2,1,0:T(8,128)} %b_hbm.1) | copy-start | bytes 3538948
  3.3 0.7 copy-start.2

commit v2 on v1

--- a/solution.py
+++ b/solution.py
@@ -10,7 +10,8 @@
 BUOYANCY = 1.0
 MESH = pl.DeviceIdType.MESH
 PAD = 8
-ROWS = 16
+ROWS = 32
+GRAM_ROWS = 16
 PAIRS = [(i, j) for j in range(4) for i in range(j + 1)]
 
 
@@ -18,7 +19,7 @@
     space,
     t_hbm,
     b_hbm,
-    diff,
+    diff_hbm,
     stepped,
     coef_out,
     y0,
@@ -32,6 +33,7 @@
     hi,
     coef,
     grams,
+    diff,
     local_sem,
     send_sem,
     recv_sem,
@@ -49,7 +51,6 @@
     has_lower = me > 0
     has_upper = me < space - 1
     ys = [y0, y1, y2, y3]
-    nu, kappa = diff[0], diff[1]
 
     def local_copies():
         out = []
@@ -113,7 +114,7 @@
         def _():
             down(*key).wait_recv()
 
-    copies = local_copies()
+    copies = local_copies() + [pltpu.make_async_copy(diff_hbm, diff, local_sem.at[2, 0])]
     for c in copies:
         c.start()
 
@@ -155,6 +156,7 @@
 
     for c in copies:
         c.wait()
+    nu, kappa = diff[0], diff[1]
 
     def x_sides(q):
         return pltpu.roll(q, nx - 1, 1), pltpu.roll(q, 1, 1)
@@ -232,20 +234,25 @@
 
     for p in inside:
         base_coeffs(0, p)
-    receive(base_up, base_down, 0)
-    for p in outside:
-        base_coeffs(0, p)
 
     which = [0, 1, 1, 2]
     for s in range(4):
-        if s == 1:
-            receive(base_up, base_down, 1)
-            for p in range(depth):
-                base_coeffs(1, p)
-        if s == 3:
-            receive(base_up, base_down, 2)
-            for p in range(depth):
-                base_coeffs(2, p)
+        early = s in (0, 3)
+        if early:
+
+            @pl.loop(0, vectors)
+            def _(j):
+                for p in inside:
+                    advance(s, which[s], j, p)
+
+        if s == 0:
+            for b in range(1, states):
+                for p in inside:
+                    base_coeffs(b, p)
+        if s != 2:
+            receive(base_up, base_down, which[s])
+            for p in outside:
+                base_coeffs(which[s], p)
 
         @pl.loop(0, vectors)
         def _(j):
@@ -254,26 +261,30 @@
                 advance(s, which[s], j, p)
             if s < 3:
                 both(send_up, send_down, s + 1, j, op="start")
-            for p in inside:
-                advance(s, which[s], j, p)
+            if not early:
+                for p in inside:
+                    advance(s, which[s], j, p)
 
         if s == 1:
             both(base_up, base_down, 2, op="start")
 
-    zero = jnp.zeros((ROWS, nx), jnp.float32)
+    zero = jnp.zeros((GRAM_ROWS, nx), jnp.float32)
     sums = (zero,) * len(PAIRS)
     for p in range(depth):
         def body(k, sums, p=p):
-            r = pl.multiple_of(k * ROWS, ROWS)
+            r = pl.multiple_of(k * GRAM_ROWS, GRAM_ROWS)
             for c in range(comps):
-                q = [stepped[j, c, p, pl.ds(r, ROWS), :] for j in range(vectors)]
+                q = [stepped[j, c, p, pl.ds(r, GRAM_ROWS), :] for j in range(vectors)]
                 sums = tuple(a + q[i] * q[j] for a, (i, j) in zip(sums, PAIRS))
             return sums
 
-        sums = lax.fori_loop(0, ny // ROWS, body, sums)
-    rows = [jnp.sum(a, axis=0, keepdims=True) for a in sums]
-    rows += [jnp.zeros((1, nx), jnp.float32)] * (16 - len(rows))
-    grams[me] = jnp.concatenate(rows, axis=0)
+        sums = lax.fori_loop(0, ny // GRAM_ROWS, body, sums)
+    lane = lax.broadcasted_iota(jnp.int32, (1, nx), 1)
+    packed = jnp.zeros((1, nx), jnp.float32)
+    for k, a in enumerate(sums):
+        whole = jnp.sum(jnp.sum(a, axis=0, keepdims=True), axis=1, keepdims=True)
+        packed = jnp.where(lane == k, whole, packed)
+    grams[me] = packed
 
     def gram_copy(d):
         return pltpu.make_async_remote_copy(
@@ -296,9 +307,13 @@
     def _(d):
         gram_arrival(d).wait_recv()
 
-    total = lax.fori_loop(0, space, lambda d, a: a + grams[d], jnp.zeros((16, nx), jnp.float32))
-    total = jnp.broadcast_to(jnp.sum(total, axis=1, keepdims=True), (16, nx))
-    gram = {pair: total[k : k + 1, :] for k, pair in enumerate(PAIRS)}
+    total = lax.fori_loop(0, space, lambda d, a: a + grams[d], jnp.zeros((1, nx), jnp.float32))
+    gram = {
+        pair: jnp.broadcast_to(
+            jnp.sum(jnp.where(lane == k, total, 0.0), axis=1, keepdims=True), (1, nx)
+        )
+        for k, pair in enumerate(PAIRS)
+    }
 
     low, inv = {}, {}
     recip = {}
@@ -375,14 +390,14 @@
     f32 = jnp.float32
     padded = ny + 2 * PAD
     vmem = pl.BlockSpec(memory_space=pltpu.VMEM)
-    hbm = pl.BlockSpec(memory_space=pl.ANY)
+    hbm = pl.BlockSpec(memory_space=pltpu.HBM)
     stepped, coef = pl.pallas_call(
         functools.partial(step_kernel, space),
         out_shape=(
             jax.ShapeDtypeStruct(tangents.shape, f32),
             jax.ShapeDtypeStruct((2 * vectors * vectors, nx), f32),
         ),
-        in_specs=[hbm, hbm, pl.BlockSpec(memory_space=pltpu.SMEM)],
+        in_specs=[hbm, hbm, hbm],
         out_specs=(vmem, vmem),
         scratch_shapes=[pltpu.VMEM((vectors, comps, depth, padded, nx), f32)] * 4
         + [
@@ -392,8 +407,9 @@
             pltpu.VMEM((4, vectors, comps, ny, nx), f32),
             pltpu.VMEM((4, vectors, comps, ny, nx), f32),
             pltpu.VMEM((states, depth, 15, ny, nx), f32),
-            pltpu.VMEM((space, 16, nx), f32),
-            pltpu.SemaphoreType.DMA((2, 3)),
+            pltpu.VMEM((space, 1, nx), f32),
+            pltpu.SMEM(diffusivity.shape, f32),
+            pltpu.SemaphoreType.DMA((3, 3)),
             pltpu.SemaphoreType.DMA((2, 4, vectors)),
             pltpu.SemaphoreType.DMA((2, 4, vectors)),
             pltpu.SemaphoreType.DMA((2, states)),
@@ -405,7 +421,7 @@
             collective_id=0, has_side_effects=True, vmem_limit_bytes=48 * 1024 * 1024
         ),
         name="tangent_step",
-    )(tangents, background, diffusivity)
+    )(*[pltpu.with_memory_space_constraint(a, pltpu.HBM) for a in (tangents, background, diffusivity)])
     block = (vectors, 1, depth, ny, nx)
     return pl.pallas_call(
         functools.partial(basis_kernel, tangents[0].size * space),

time: 74.9 us -> 69.3 us (0.925)
  local copies, waits for them, and re-layouts: 3.33 us -> 0 us
  Pallas kernels: 70.8 us -> 68.5 us
    unnamed x6 -> x0, local copies, waits for them, and re-layouts: 3.33 us -> none
    pallas_call x1, Pallas kernels: 69 us -> 66.8 us  [on_device(): pl.pallas_call(functools.partial(step_kernel, space), out_shape=(jax.Shap...]
where the time goes in v2:
time: 69.3 us; the launch traced here: 69.2 us
  Pallas kernels  68.5 us (99%)
    pallas_call x1, Pallas kernels, on_device(): pl.pallas_call(functools.partial(step_kernel, space), out_shape=(jax.Shap...  66.8 us
    pallas_call x1, Pallas kernels, on_device(): pl.pallas_call(functools.partial(basis_kernel, tangents[0].size * space),...  1.77 us

profile of v2, /device:TPU:0, one launch (start us, length us, event | category | flops | bytes accessed | tf_op | source)
XLA Modules:
  0.0 69.2 jit_solution(8545127342765631538)
XLA Ops:
  0.6 66.8 %tangent_step.1 = (f32[4,4,3,64,128]{4,3,2,1,0:T(8,128)S(1)}, f32[32,128]{1,0:T(8,128)S(1)}) custom-call(f32[4,4,3,64,128]{4,3,2,1,0:T(8,128)} %t_hbm.1, f32[3,4,3,64,128]{4,3,2,1,0:T(8,128)} %b_hbm.1, f32[2]{0:T(128)} %diff_hbm.1), custom_call_target="tpu_custom_call" | custom-call | tf_op jit(solution)/shard_map/tangent_step/pallas_call | solution.py:394
  67.4 1.8 %basis.1 = (f32[4,4,3,64,128]{4,3,2,1,0:T(8,128)}, f32[4,4]{1,0:T(4,128)}) custom-call(f32[4,4,3,64,128]{4,3,2,1,0:T(8,128)S(1)} %get-tuple-element.4.stepped, f32[32,128]{1,0:T(8,128)S(1)} %get-tuple-element.5.coef), custom_call_target="tpu_custom_call" | custom-call | tf_op jit(solution)/shard_map/basis/pallas_call | solution.py:426

commit v3 on v2

--- a/solution.py
+++ b/solution.py
@@ -10,6 +10,7 @@
 BUOYANCY = 1.0
 MESH = pl.DeviceIdType.MESH
 PAD = 8
+GROUP = 4
 ROWS = 32
 GRAM_ROWS = 16
 PAIRS = [(i, j) for j in range(4) for i in range(j + 1)]
@@ -34,6 +35,8 @@
     coef,
     grams,
     diff,
+    relay,
+    base_relay,
     local_sem,
     send_sem,
     recv_sem,
@@ -41,6 +44,10 @@
     base_recv,
     gram_send,
     gram_recv,
+    relay_send,
+    relay_recv,
+    base_relay_send,
+    base_relay_recv,
 ):
     vectors, comps, depth, ny, nx = t_hbm.shape
     states = b_hbm.shape[0]
@@ -51,6 +58,16 @@
     has_lower = me > 0
     has_upper = me < space - 1
     ys = [y0, y1, y2, y3]
+
+    relays = space % GROUP == 0 and space <= GROUP * GROUP
+    groups = max(space // GROUP, 1)
+    group, seat = lax.div(me, GROUP), lax.rem(me, GROUP)
+
+    def via_up(items):
+        return lax.div(items * (groups - 1 - group), groups)
+
+    def via_down(items):
+        return lax.div(items * group, groups)
 
     def local_copies():
         out = []
@@ -67,45 +84,105 @@
                 )
         return out
 
-    def base_up(b):
+    def remote(src, dst, sems, device):
         return pltpu.make_async_remote_copy(
-            b_hbm.at[b, :, last], base_lo.at[b], base_send.at[0, b], base_recv.at[0, b],
-            device_id={"space": upper}, device_id_type=MESH,
+            src, dst, sems[0], sems[1], device_id={"space": device}, device_id_type=MESH
         )
 
-    def base_down(b):
-        return pltpu.make_async_remote_copy(
-            b_hbm.at[b, :, 0], base_hi.at[b], base_send.at[1, b], base_recv.at[1, b],
-            device_id={"space": lower}, device_id_type=MESH,
-        )
+    around = [lax.rem(me + space + k, space) for k in (-2, 2, 3, -3)]
+
+    def base_up(b, via=False):
+        dst, sem = (base_relay, base_relay_recv.at[b]) if via else (base_lo, base_recv.at[0, b])
+        device = around[0] if via else upper
+        return remote(b_hbm.at[b, :, last], dst.at[b], (base_send.at[0, b], sem), device)
+
+    def base_down(b, via=False):
+        dst, sem = (base_relay, base_relay_recv.at[b]) if via else (base_hi, base_recv.at[1, b])
+        device = around[1] if via else lower
+        return remote(b_hbm.at[b, :, 0], dst.at[b], (base_send.at[1, b], sem), device)
 
     def state_plane(s, j, p):
         if s == 0:
             return t_hbm.at[j, :, p]
         return ys[s].at[j, :, p, pl.ds(PAD, ny), :]
 
-    def send_up(s, j):
-        return pltpu.make_async_remote_copy(
-            state_plane(s, j, last), lo.at[s, j], send_sem.at[0, s, j], recv_sem.at[0, s, j],
-            device_id={"space": upper}, device_id_type=MESH,
+    def send_up(s, j, via=False):
+        dst, sem = (relay, relay_recv.at[s, j]) if via else (lo, recv_sem.at[0, s, j])
+        device = around[0] if via else upper
+        return remote(
+            state_plane(s, j, last), dst.at[s, j], (send_sem.at[0, s, j], sem), device
         )
 
-    def send_down(s, j):
-        return pltpu.make_async_remote_copy(
-            state_plane(s, j, 0), hi.at[s, j], send_sem.at[1, s, j], recv_sem.at[1, s, j],
-            device_id={"space": lower}, device_id_type=MESH,
-        )
-
-    def both(up, down, *key, op):
+    def send_down(s, j, via=False):
+        dst, sem = (relay, relay_recv.at[s, j]) if via else (hi, recv_sem.at[1, s, j])
+        device = around[1] if via else lower
+        return remote(state_plane(s, j, 0), dst.at[s, j], (send_sem.at[1, s, j], sem), device)
+
+    def start(up, down, *key):
+        items = states if len(key) == 1 else vectors
+        if relays:
+            around_up = jnp.logical_and(seat == GROUP - 1, key[-1] < via_up(items))
+            around_down = jnp.logical_and(seat == 0, key[-1] < via_down(items))
+
+            @pl.when(around_up)
+            def _():
+                up(*key, via=True).start()
+
+            @pl.when(around_down)
+            def _():
+                down(*key, via=True).start()
+
+            straight_up = jnp.logical_and(has_upper, jnp.logical_not(around_up))
+            straight_down = jnp.logical_and(has_lower, jnp.logical_not(around_down))
+        else:
+            straight_up, straight_down = has_upper, has_lower
+
+        @pl.when(straight_up)
+        def _():
+            up(*key).start()
+
+        @pl.when(straight_down)
+        def _():
+            down(*key).start()
+
+    def passes(*key, op):
+        if not relays:
+            return
+        if len(key) == 1:
+            items, held, sends, arrivals = states, base_relay, base_relay_send, base_relay_recv
+            ends, ends_recv = (base_lo, base_hi), base_recv
+        else:
+            items, held, sends, arrivals = vectors, relay, relay_send, relay_recv
+            ends, ends_recv = (lo, hi), recv_sem
+        for side, (place, count) in enumerate(((1, via_up(items)), (2, via_down(items)))):
+
+            @pl.when(jnp.logical_and(seat == place, key[-1] < count))
+            def _():
+                src = held.at[key]
+                onward = remote(
+                    src, ends[side].at[key], (sends.at[key], ends_recv.at[(side, *key)]),
+                    around[2 + side],
+                )
+                if op == "start":
+                    remote(src, src, (sends.at[key], arrivals.at[key]), upper).wait_recv()
+                    onward.start()
+                else:
+                    onward.wait_send()
+
+    def sent(up, down, *key):
         @pl.when(has_upper)
         def _():
-            getattr(up(*key), op)()
+            up(*key).wait_send()
 
         @pl.when(has_lower)
         def _():
-            getattr(down(*key), op)()
+            down(*key).wait_send()
+
+        passes(*key, op="wait_send")
 
     def receive(up, down, *key):
+        passes(*key, op="start")
+
         @pl.when(has_lower)
         def _():
             up(*key).wait_recv()
@@ -128,13 +205,13 @@
 
     pl.semaphore_wait(barrier, space - 1)
 
-    both(base_up, base_down, 0, op="start")
+    start(base_up, base_down, 0)
 
     @pl.loop(0, vectors)
     def _(j):
-        both(send_up, send_down, 0, j, op="start")
-
-    both(base_up, base_down, 1, op="start")
+        start(send_up, send_down, 0, j)
+
+    start(base_up, base_down, 1)
 
     @pl.when(jnp.logical_not(has_lower))
     def _():
@@ -207,16 +284,16 @@
                 )
                 for d in range(3):
                     rate = rate + qs[d] * coef[b, p, 3 + 3 * c + d, here, :]
-                around = (right + left) + (front + back) + (above + below)
-                rate = rate + (kappa if c == 3 else nu) * (around - 6.0 * q)
+                sides = (right + left) + (front + back) + (above + below)
+                rate = rate + (kappa if c == 3 else nu) * (sides - 6.0 * q)
                 if c == 2:
                     rate = rate + BUOYANCY * qs[3]
                 if c == 3:
                     rate = rate + qs[2]
                 if s < 3:
-                    start = q if s == 0 else y0[j, c, p, mid, :]
+                    origin = q if s == 0 else y0[j, c, p, mid, :]
                     step = STEP_DT if s == 2 else STEP_DT * 0.5
-                    ys[s + 1][j, c, p, mid, :] = start + step * rate
+                    ys[s + 1][j, c, p, mid, :] = origin + step * rate
                 else:
                     sums = (
                         y1[j, c, p, mid, :] + 2.0 * y2[j, c, p, mid, :] + (q - y0[j, c, p, mid, :])
@@ -260,13 +337,13 @@
             for p in outside:
                 advance(s, which[s], j, p)
             if s < 3:
-                both(send_up, send_down, s + 1, j, op="start")
+                start(send_up, send_down, s + 1, j)
             if not early:
                 for p in inside:
                     advance(s, which[s], j, p)
 
         if s == 1:
-            both(base_up, base_down, 2, op="start")
+            start(base_up, base_down, 2)
 
     zero = jnp.zeros((GRAM_ROWS, nx), jnp.float32)
     sums = (zero,) * len(PAIRS)
@@ -341,11 +418,11 @@
     coef_out[...] = jnp.concatenate(rows, axis=0)
 
     for b in range(states):
-        both(base_up, base_down, b, op="wait_send")
+        sent(base_up, base_down, b)
     for s in range(4):
         @pl.loop(0, vectors)
         def _(j):
-            both(send_up, send_down, s, j, op="wait_send")
+            sent(send_up, send_down, s, j)
 
     @pl.loop(1, space)
     def _(d):
@@ -409,6 +486,8 @@
             pltpu.VMEM((states, depth, 15, ny, nx), f32),
             pltpu.VMEM((space, 1, nx), f32),
             pltpu.SMEM(diffusivity.shape, f32),
+            pltpu.VMEM((4, vectors, comps, ny, nx), f32),
+            pltpu.VMEM((states, comps, ny, nx), f32),
             pltpu.SemaphoreType.DMA((3, 3)),
             pltpu.SemaphoreType.DMA((2, 4, vectors)),
             pltpu.SemaphoreType.DMA((2, 4, vectors)),
@@ -416,6 +495,10 @@
             pltpu.SemaphoreType.DMA((2, states)),
             pltpu.SemaphoreType.DMA((space,)),
             pltpu.SemaphoreType.DMA((space,)),
+            pltpu.SemaphoreType.DMA((4, vectors)),
+            pltpu.SemaphoreType.DMA((4, vectors)),
+            pltpu.SemaphoreType.DMA((states,)),
+            pltpu.SemaphoreType.DMA((states,)),
         ],
         compiler_params=pltpu.CompilerParams(
             collective_id=0, has_side_effects=True, vmem_limit_bytes=48 * 1024 * 1024

time: 69.3 us -> 64.2 us (0.926)
  Pallas kernels: 68.5 us -> 63.4 us
    pallas_call x1, Pallas kernels: 66.8 us -> 61.6 us  [on_device(): pl.pallas_call(functools.partial(step_kernel, space), out_shape=(jax.Shap...]
where the time goes in v3:
time: 64.2 us; the launch traced here: 64 us
  Pallas kernels  63.4 us (99%)
    pallas_call x1, Pallas kernels, on_device(): pl.pallas_call(functools.partial(step_kernel, space), out_shape=(jax.Shap...  61.6 us
    pallas_call x1, Pallas kernels, on_device(): pl.pallas_call(functools.partial(basis_kernel, tangents[0].size * space),...  1.77 us

profile of v3, /device:TPU:0, one launch (start us, length us, event | category | flops | bytes accessed | tf_op | source)
XLA Modules:
  0.0 64.0 jit_solution(9460928817832163202)
XLA Ops:
  0.6 61.6 %tangent_step.1 = (f32[4,4,3,64,128]{4,3,2,1,0:T(8,128)S(1)}, f32[32,128]{1,0:T(8,128)S(1)}) custom-call(f32[4,4,3,64,128]{4,3,2,1,0:T(8,128)} %t_hbm.1, f32[3,4,3,64,128]{4,3,2,1,0:T(8,128)} %b_hbm.1, f32[2]{0:T(128)} %diff_hbm.1), custom_call_target="tpu_custom_call" | custom-call | tf_op jit(solution)/shard_map/tangent_step/pallas_call | solution.py:471
  62.3 1.8 %basis.1 = (f32[4,4,3,64,128]{4,3,2,1,0:T(8,128)}, f32[4,4]{1,0:T(4,128)}) custom-call(f32[4,4,3,64,128]{4,3,2,1,0:T(8,128)S(1)} %get-tuple-element.4.stepped, f32[32,128]{1,0:T(8,128)S(1)} %get-tuple-element.5.coef), custom_call_target="tpu_custom_call" | custom-call | tf_op jit(solution)/shard_map/basis/pallas_call | solution.py:509

commit v4 on v3

--- a/solution.py
+++ b/solution.py
@@ -211,8 +211,6 @@
     def _(j):
         start(send_up, send_down, 0, j)
 
-    start(base_up, base_down, 1)
-
     @pl.when(jnp.logical_not(has_lower))
     def _():
         base_lo[...] = jnp.zeros_like(base_lo)
@@ -326,12 +324,13 @@
             for b in range(1, states):
                 for p in inside:
                     base_coeffs(b, p)
+            start(base_up, base_down, 1)
         if s != 2:
             receive(base_up, base_down, which[s])
             for p in outside:
                 base_coeffs(which[s], p)
 
-        @pl.loop(0, vectors)
+        @pl.loop(0, vectors if s < 3 else vectors - 1)
         def _(j):
             receive(send_up, send_down, s, j)
             for p in outside:
@@ -345,17 +344,30 @@
         if s == 1:
             start(base_up, base_down, 2)
 
+    def inner_products(planes, pairs, sums):
+        for p in planes:
+
+            def body(k, sums, p=p):
+                r = pl.multiple_of(k * GRAM_ROWS, GRAM_ROWS)
+                for c in range(comps):
+                    used = sorted({j for pair in pairs for j in pair})
+                    q = {j: stepped[j, c, p, pl.ds(r, GRAM_ROWS), :] for j in used}
+                    sums = tuple(a + q[i] * q[j] for a, (i, j) in zip(sums, pairs))
+                return sums
+
+            sums = lax.fori_loop(0, ny // GRAM_ROWS, body, sums)
+        return sums
+
     zero = jnp.zeros((GRAM_ROWS, nx), jnp.float32)
-    sums = (zero,) * len(PAIRS)
-    for p in range(depth):
-        def body(k, sums, p=p):
-            r = pl.multiple_of(k * GRAM_ROWS, GRAM_ROWS)
-            for c in range(comps):
-                q = [stepped[j, c, p, pl.ds(r, GRAM_ROWS), :] for j in range(vectors)]
-                sums = tuple(a + q[i] * q[j] for a, (i, j) in zip(sums, PAIRS))
-            return sums
-
-        sums = lax.fori_loop(0, ny // GRAM_ROWS, body, sums)
+    first = [pair for pair in PAIRS if pair[1] < vectors - 1]
+    final = [pair for pair in PAIRS if pair[1] == vectors - 1]
+    sums = inner_products(range(depth), first, (zero,) * len(first))
+    late = inner_products(inside, final, (zero,) * len(final))
+    receive(send_up, send_down, 3, vectors - 1)
+    for p in outside:
+        advance(3, which[3], vectors - 1, p)
+    sums = sums + inner_products(outside, final, late)
+
     lane = lax.broadcasted_iota(jnp.int32, (1, nx), 1)
     packed = jnp.zeros((1, nx), jnp.float32)
     for k, a in enumerate(sums):

time: 64.2 us -> 64.1 us (level)
  no operation moved by 1% of the time
where the time goes in v4:
time: 64.1 us; the launch traced here: 63.9 us
  Pallas kernels  63.3 us (99%)
    pallas_call x1, Pallas kernels, on_device(): pl.pallas_call(functools.partial(step_kernel, space), out_shape=(jax.Shap...  61.5 us
    pallas_call x1, Pallas kernels, on_device(): pl.pallas_call(functools.partial(basis_kernel, tangents[0].size * space),...  1.77 us

profile of v4, /device:TPU:0, one launch (start us, length us, event | category | flops | bytes accessed | tf_op | source)
XLA Modules:
  0.0 63.9 jit_solution(5118285724261374572)
XLA Ops:
  0.6 61.5 %tangent_step.1 = (f32[4,4,3,64,128]{4,3,2,1,0:T(8,128)S(1)}, f32[32,128]{1,0:T(8,128)S(1)}) custom-call(f32[4,4,3,64,128]{4,3,2,1,0:T(8,128)} %t_hbm.1, f32[3,4,3,64,128]{4,3,2,1,0:T(8,128)} %b_hbm.1, f32[2]{0:T(128)} %diff_hbm.1), custom_call_target="tpu_custom_call" | custom-call | tf_op jit(solution)/shard_map/tangent_step/pallas_call | solution.py:483
  62.2 1.8 %basis.1 = (f32[4,4,3,64,128]{4,3,2,1,0:T(8,128)}, f32[4,4]{1,0:T(4,128)}) custom-call(f32[4,4,3,64,128]{4,3,2,1,0:T(8,128)S(1)} %get-tuple-element.4.stepped, f32[32,128]{1,0:T(8,128)S(1)} %get-tuple-element.5.coef), custom_call_target="tpu_custom_call" | custom-call | tf_op jit(solution)/shard_map/basis/pallas_call | solution.py:521

commit v5 on v4

--- a/solution.py
+++ b/solution.py
@@ -118,32 +118,40 @@
         device = around[1] if via else lower
         return remote(state_plane(s, j, 0), dst.at[s, j], (send_sem.at[1, s, j], sem), device)
 
-    def start(up, down, *key):
+    def start(up, down, *key, sides=("up", "down")):
         items = states if len(key) == 1 else vectors
         if relays:
             around_up = jnp.logical_and(seat == GROUP - 1, key[-1] < via_up(items))
             around_down = jnp.logical_and(seat == 0, key[-1] < via_down(items))
 
-            @pl.when(around_up)
-            def _():
-                up(*key, via=True).start()
-
-            @pl.when(around_down)
-            def _():
-                down(*key, via=True).start()
+            if "up" in sides:
+
+                @pl.when(around_up)
+                def _():
+                    up(*key, via=True).start()
+
+            if "down" in sides:
+
+                @pl.when(around_down)
+                def _():
+                    down(*key, via=True).start()
 
             straight_up = jnp.logical_and(has_upper, jnp.logical_not(around_up))
             straight_down = jnp.logical_and(has_lower, jnp.logical_not(around_down))
         else:
             straight_up, straight_down = has_upper, has_lower
 
-        @pl.when(straight_up)
-        def _():
-            up(*key).start()
-
-        @pl.when(straight_down)
-        def _():
-            down(*key).start()
+        if "up" in sides:
+
+            @pl.when(straight_up)
+            def _():
+                up(*key).start()
+
+        if "down" in sides:
+
+            @pl.when(straight_down)
+            def _():
+                down(*key).start()
 
     def passes(*key, op):
         if not relays:
@@ -180,16 +188,20 @@
 
         passes(*key, op="wait_send")
 
-    def receive(up, down, *key):
-        passes(*key, op="start")
-
+    def receive_low(up, *key):
         @pl.when(has_lower)
         def _():
             up(*key).wait_recv()
 
+    def receive_high(down, *key):
         @pl.when(has_upper)
         def _():
             down(*key).wait_recv()
+
+    def receive(up, down, *key):
+        passes(*key, op="start")
+        receive_low(up, *key)
+        receive_high(down, *key)
 
     copies = local_copies() + [pltpu.make_async_copy(diff_hbm, diff, local_sem.at[2, 0])]
     for c in copies:
@@ -311,6 +323,24 @@
         base_coeffs(0, p)
 
     which = [0, 1, 1, 2]
+
+    def outer(s, j):
+        if last == 0:
+            receive(send_up, send_down, s, j)
+            advance(s, which[s], j, 0)
+            if s < 3:
+                start(send_up, send_down, s + 1, j)
+            return
+        passes(s, j, op="start")
+        receive_low(send_up, s, j)
+        advance(s, which[s], j, 0)
+        if s < 3:
+            start(send_up, send_down, s + 1, j, sides=("down",))
+        receive_high(send_down, s, j)
+        advance(s, which[s], j, last)
+        if s < 3:
+            start(send_up, send_down, s + 1, j, sides=("up",))
+
     for s in range(4):
         early = s in (0, 3)
         if early:
@@ -332,11 +362,7 @@
 
         @pl.loop(0, vectors if s < 3 else vectors - 1)
         def _(j):
-            receive(send_up, send_down, s, j)
-            for p in outside:
-                advance(s, which[s], j, p)
-            if s < 3:
-                start(send_up, send_down, s + 1, j)
+            outer(s, j)
             if not early:
                 for p in inside:
                     advance(s, which[s], j, p)
@@ -363,9 +389,7 @@
     final = [pair for pair in PAIRS if pair[1] == vectors - 1]
     sums = inner_products(range(depth), first, (zero,) * len(first))
     late = inner_products(inside, final, (zero,) * len(final))
-    receive(send_up, send_down, 3, vectors - 1)
-    for p in outside:
-        advance(3, which[3], vectors - 1, p)
+    outer(3, vectors - 1)
     sums = sums + inner_products(outside, final, late)
 
     lane = lax.broadcasted_iota(jnp.int32, (1, nx), 1)

time: 64.1 us -> 64 us (level)
  no operation moved by 1% of the time
where the time goes in v5:
time: 64 us; the launch traced here: 63.8 us
  Pallas kernels  63.2 us (99%)
  between operations  0.64 us (1%)
    pallas_call x1, Pallas kernels, on_device(): pl.pallas_call(functools.partial(step_kernel, space), out_shape=(jax.Shap...  61.4 us
    pallas_call x1, Pallas kernels, on_device(): pl.pallas_call(functools.partial(basis_kernel, tangents[0].size * space),...  1.77 us

profile of v5, /device:TPU:0, one launch (start us, length us, event | category | flops | bytes accessed | tf_op | source)
XLA Modules:
  0.0 63.8 jit_solution(8737410841703363029)
XLA Ops:
  0.6 61.4 %tangent_step.1 = (f32[4,4,3,64,128]{4,3,2,1,0:T(8,128)S(1)}, f32[32,128]{1,0:T(8,128)S(1)}) custom-call(f32[4,4,3,64,128]{4,3,2,1,0:T(8,128)} %t_hbm.1, f32[3,4,3,64,128]{4,3,2,1,0:T(8,128)} %b_hbm.1, f32[2]{0:T(128)} %diff_hbm.1), custom_call_target="tpu_custom_call" | custom-call | tf_op jit(solution)/shard_map/tangent_step/pallas_call | solution.py:507
  62.0 1.8 %basis.1 = (f32[4,4,3,64,128]{4,3,2,1,0:T(8,128)}, f32[4,4]{1,0:T(4,128)}) custom-call(f32[4,4,3,64,128]{4,3,2,1,0:T(8,128)S(1)} %get-tuple-element.4.stepped, f32[32,128]{1,0:T(8,128)S(1)} %get-tuple-element.5.coef), custom_call_target="tpu_custom_call" | custom-call | tf_op jit(solution)/shard_map/basis/pallas_call | solution.py:545
